TPU v7x, 256 devices: a whole 4x4x8 slice. The times are simulated.
256 devices in a mesh: row: 8 (over y_hi, x), col: 32 (over y_lo, z, core).
Axes of the slice: x: 4, y: 4 (y_hi: 2, y_lo: 2; y = y_hi * 2 + y_lo), z: 8, core: 2. Of those that a mesh axis runs over, the one named last changes fastest.
Arguments:
- vectors: float32 [16384, 8192], P('row', 'col'), may hold values from -6 to 6
- panels: float32 [32, 16384, 256], P('col', 'row'), may hold values from -0.046875 to 0.046875
- factors: float32 [3, 256, 256], replicated, as said below
- owners: int32 [3], replicated, may hold values from 0 to 31
Outputs:
- updated: float32 [16384, 8192], P('row', 'col')
Inputs may be any that keep to these rules, and one draw needn't show every extreme that they name: Each factors[k] is upper triangular with a positive diagonal. owners may repeat.
All inputs are finite; a program needn't handle non-finite values.
Results may differ from a plain program's by a relative error of at most 0.0002.
Values sent between devices are 32-bit elements; how exact they have to be, the bound alone decides.
A program may use at most 64 MiB of HBM per device.

v0:
```python
import jax
import jax.numpy as jnp
from jax import lax
from jax.sharding import PartitionSpec as P

BLOCKS = 3


def spread(value, axis, source):
    kept = jnp.where(lax.axis_index(axis) == source, value, 0).astype(value.dtype)
    return lax.psum(kept, axis)


def inner(left, right):
    return lax.dot_general(
        left,
        right,
        (((0,), (0,)), ((), ())),
        precision=lax.Precision.HIGHEST,
        preferred_element_type=jnp.float32,
    )


def matmul(left, right):
    return jnp.dot(left, right, precision=lax.Precision.HIGHEST, preferred_element_type=jnp.float32)


def fetch(panels, owners, block):
    return spread(panels[0], "col", owners[block])


def shards(vectors, panels, factors, owners):
    current = vectors
    for block in range(BLOCKS):
        reflector = fetch(panels, owners, block)
        projected = lax.psum(inner(reflector, current), "row")
        scaled = matmul(factors[block], projected)
        current = current - matmul(reflector, scaled)
    return current


def solution(mesh):
    placed = (P("row", "col"), P("col", "row", None), P(), P())
    return jax.shard_map(
        shards, mesh=mesh, in_specs=placed, out_specs=P("row", "col"), check_vma=False
    )
```

profile of v0, /device:TPU:1, one launch (start us, length us, event | category | flops | bytes accessed | tf_op | source)
XLA Modules:
  0.0 557.6 jit_solution(13413525478540377163)
XLA Ops:
  6.5 0.0 all-reduce.12.cloned.1.call-start
  6.5 1.4 fusion.9
  9.9 4.5 select_bitcast_fusion
  14.3 0.0 all-reduce.12.cloned.1.call-update
  14.4 0.0 all-reduce.6.cloned.1.call-start
  14.4 245.0 %all-reduce.12.cloned.1.call-done = (f32[2048,256]{1,0:T(8,128)}, f32[2048,256]{1,0:T(8,128)}, f32[2048,256]{1,0:T(8,128)}) async-done(((f32[2048,256]{1,0:T(8,128)}, f32[2048,256]{1,0:T(8,128)}, f32[2048,256]{1,0:T(8,128)}), (f32[2048,256]{1,0:T(8,128)}, f32[2048,256]{1,0:T(8,128)}, f32[2048,256]{1,0:T(8,128)})) %all-reduce.12.cloned.1.call-update) | async-done | bytes 6291472 | tf_op jit(solution)/shard_map/psum | solution.py:11
  259.4 0.0 copy-done.1
  259.4 5.8 %fusion.10 = f32[256,256]{1,0:T(8,128)} fusion(f32[2048,256]{1,0:T(8,128)} %get-tuple-element.5, f32[2048,256]{1,0:T(8,128)S(1)} %copy-done.1), kind=kOutput, calls=%fused_computation.16 | convolution fusion | flops 1610612736 | bytes 4456448 | tf_op jit(solution)/shard_map/dot_general | solution.py:15
  265.2 0.0 all-reduce.6.cloned.1.call-update
  265.2 0.0 all-reduce.8.cloned.1.call-start
  265.3 83.0 %all-reduce.6.cloned.1.call-done = f32[256,256]{1,0:T(8,128)} async-done(((f32[256,256]{1,0:T(8,128)}), f32[256,256]{1,0:T(8,128)}) %all-reduce.6.cloned.1.call-update) | async-done | bytes 262160 | tf_op jit(solution)/shard_map/psum | solution.py:36
  348.2 0.0 copy-done.5
  348.3 1.5 fusion.4
  349.8 0.0 copy-start.4
  349.8 4.2 convolution_subtract_fusion.2
  354.0 0.0 copy-done.4
  354.0 4.3 fusion.11
  358.4 0.0 all-reduce.8.cloned.1.call-update
  358.4 0.2 all-reduce.10.cloned.1.call-start
  358.6 87.5 %all-reduce.8.cloned.1.call-done = f32[256,256]{1,0:T(8,128)} async-done(((f32[256,256]{1,0:T(8,128)}), f32[256,256]{1,0:T(8,128)}) %all-reduce.8.cloned.1.call-update) | async-done | bytes 262160 | tf_op jit(solution)/shard_map/psum | solution.py:36
  446.1 1.5 fusion.2
  447.7 0.0 copy-start.2
  447.7 3.6 convolution_subtract_fusion.1
  451.3 0.0 copy-start
  451.3 1.3 copy-done
  452.6 0.0 copy-done.2
  452.7 4.3 fusion.12
  457.0 0.0 all-reduce.10.cloned.1.call-update
  457.0 87.7 %all-reduce.10.cloned.1.call-done = f32[256,256]{1,0:T(8,128)} async-done(((f32[256,256]{1,0:T(8,128)}), f32[256,256]{1,0:T(8,128)}) %all-reduce.10.cloned.1.call-update) | async-done | bytes 262160 | tf_op jit(solution)/shard_map/psum | solution.py:36
  544.7 1.5 fusion
  546.3 0.0 copy-done.3
  546.3 4.7 convolution_subtract_fusion
  (3 shorter events, 0.0 us)
Async XLA Ops:
  6.5 252.8 %all-reduce.12.cloned.1.call-start = ((), (), s32[]{:S(2)}) async-start(), calls=%async_computation.3 | async-start | bytes 12582912 | tf_op jit(solution)/shard_map/psum | solution.py:11
  14.3 245.1 %copy-start.1 = (f32[2048,256]{1,0:T(8,128)S(1)}, f32[2048,256]{1,0:T(8,128)}, u32[]{:S(2)}) copy-start(f32[2048,256]{1,0:T(8,128)} %param.4) | copy-start | bytes 6291460
  14.4 333.9 %all-reduce.6.cloned.1.call-start = ((), (), s32[]{:S(2)}) async-start(), calls=%async_computation | async-start | bytes 524288 | tf_op jit(solution)/shard_map/psum | solution.py:36
  259.4 88.9 %copy-start.5 = (f32[3,256,256]{2,1,0:T(8,128)S(1)}, f32[3,256,256]{2,1,0:T(8,128)}, u32[]{:S(2)}) copy-start(f32[3,256,256]{2,1,0:T(8,128)} %param.6) | copy-start | bytes 2359300
  265.2 180.9 %all-reduce.8.cloned.1.call-start = ((), (), s32[]{:S(2)}) async-start(), calls=%async_computation.1 | async-start | bytes 524288 | tf_op jit(solution)/shard_map/psum | solution.py:36
  349.8 4.2 copy-start.4
  358.4 186.4 %all-reduce.10.cloned.1.call-start = ((), (), s32[]{:S(2)}) async-start(), calls=%async_computation.2 | async-start | bytes 524288 | tf_op jit(solution)/shard_map/psum | solution.py:36
  447.7 5.0 copy-start.2
  451.3 1.3 copy-start
  452.6 93.6 %copy-start.3 = (f32[2048,256]{1,0:T(8,128)S(1)}, f32[2048,256]{1,0:T(8,128)}, u32[]{:S(2)}) copy-start(f32[2048,256]{1,0:T(8,128)} %get-tuple-element.7) | copy-start | bytes 6291460
Sparse Core Ops, SparseCore 0:
  14.5 244.8 all-reduce.11
  265.4 82.8 all-reduce.5
  358.5 87.5 all-reduce.7
  457.1 87.5 all-reduce.9
where the time goes:
time: 562 us; the launch traced here: 558 us
  waiting for transfers between devices  503 us (90%)
  matrix products  31.7 us (6%)
  between operations  15.1 us (3%)
    psum x3, waiting for transfers between devices, shards(): projected = lax.psum(inner(reflector, current), 'row')  258 us
    psum x1, waiting for transfers between devices, spread(): return lax.psum(kept, axis)  245 us
    dot_general x6, matrix products, matmul(): jnp.dot(left, right, precision=lax.Precision.HIGHEST, preferred_element_t...  17.2 us
    dot_general x3, matrix products, inner(): lax.dot_general(left, right, (((0,), (0,)), ((), ())), precision=lax.Prec...  14.5 us
  transfers between devices with their start and end apart: 4, of which 4 were waited for; matrix products, arithmetic and copies ran while one was open for 0% of the time, Pallas kernels for 0%

commit v1 on v0

v1 whole, which is shorter than its diff:
```python
import functools

import jax
import jax.numpy as jnp
from jax import lax
from jax.experimental import pallas as pl
from jax.experimental.pallas import tpu as pltpu
from jax.sharding import PartitionSpec as P

MESH = pl.DeviceIdType.MESH
F32, BF16 = jnp.float32, jnp.bfloat16
BLOCKS = 3
WIDTH = 256
HALF = WIDTH // 2
ROWS = 2048
GROUP = 256
CHUNK = 512
UNIT = 64
PIECES = (64, 32)
ORDER = (4, -3, 3, -2, 2, -1, 1, 0)
LONG, SHORT = 4, 3
HOPS = (LONG, SHORT)
SHARES = (32, 48, 64)
LAGS = (0, 0, 0)
NN = (((1,), (0,)), ((), ()))
NT = (((1,), (1,)), ((), ()))


def halves(x):
    high = x.astype(BF16)
    return high, (x - high.astype(F32)).astype(BF16)


def dot3(a, b, dims=NN):
    def one(p, q):
        return lax.dot_general(p, q, dims, preferred_element_type=F32)

    return one(a[0], b[0]) + (one(a[0], b[1]) + one(a[1], b[0]))


def kernel(
    owners, c_ref, panel_ref, factors_ref, o_ref,
    c_v, f_v, left_hi, left_lo, v0, v1, v2, v_hi, v_lo,
    own_a, own_b, got_a, got_b, mine_a, mine_b, passed_a, passed_b, half_a, other_a,
    part0, part1, part2, sum0, sum1, sum2, in0, in1, in2, gram1, gram2, yt_hi, yt_lo, y_hi, y_lo,
    local_sem, first_s, first_r, rs_s, rs_r, beside_s, beside_r, ag_s, ag_r, side_s, side_r, core_s, core_r, row_s, row_r,
    gram_s, gram_r,
):
    v, part, total, arrived = (v0, v1, v2), (part0, part1, part2), (sum0, sum1, sum2), (in0, in1, in2)
    gram = (None, gram1, gram2)
    mine, passed = (mine_a, mine_b), (passed_a, passed_b)
    row, col = lax.axis_index("row"), lax.axis_index("col")
    yh, x = row // 4, row % 4
    yl, z, h = col // 16, (col // 2) % 8, col % 2
    sign = 1 - 2 * h

    def along(where):
        return lax.rem(z + 8 + where, 8)

    def at(dyl, dz, dh):
        return (row, (yl ^ dyl) * 16 + along(dz) * 2 + (h ^ dh))

    def unit_rows(u, half, where):
        return pl.ds(pl.multiple_of(along(where) * GROUP + half * (GROUP // 2) + u * UNIT, UNIT), UNIT)

    def small_rows(half, y, where):
        start = along(where) * GROUP + half * (GROUP // 2) + UNIT + y * PIECES[1]
        return pl.ds(pl.multiple_of(start, PIECES[1]), PIECES[1])

    def group_rows(where):
        return pl.ds(pl.multiple_of(along(where) * GROUP, GROUP), GROUP)

    def remote(src, dst, send, recv, device):
        return pltpu.make_async_remote_copy(
            src_ref=src, dst_ref=dst, send_sem=send, recv_sem=recv, device_id=device, device_id_type=MESH
        )

    sibling, partner, diagonal = at(0, 0, 1), at(1, 0, 0), at(1, 0, 1)
    ahead, behind = at(0, sign, 0), at(0, -sign, 0)
    peers = [((yh ^ (i // 4)) * 4 + (x + i % 4) % 4, col) for i in range(1, 8)]

    barrier = pltpu.get_barrier_semaphore()
    everyone = [sibling, partner, diagonal, ahead, behind] + peers
    for device in everyone:
        pl.semaphore_signal(barrier, inc=1, device_id=device, device_id_type=MESH)

    load_c = pltpu.make_async_copy(c_ref, c_v, local_sem.at[0])
    load_f = pltpu.make_async_copy(factors_ref, f_v, local_sem.at[1])
    loads = []
    for i, rel in enumerate(ORDER):
        where = sign * rel
        loads.append(
            (
                pltpu.make_async_copy(panel_ref.at[unit_rows(0, h, where)], own_a.at[i], local_sem.at[2 + i]),
                pltpu.make_async_copy(panel_ref.at[small_rows(h, yl, where)], own_b.at[i], local_sem.at[10 + i]),
            )
        )
        for load in loads[-1]:
            load.start()
    load_c.start()
    load_f.start()

    held = (col, col ^ 16, col ^ 17, col ^ 1)
    weight = [[jnp.where(owners[k] == c, 1.0, 0.0).astype(F32) for c in held] for k in range(BLOCKS)]

    pl.semaphore_wait(barrier, len(everyone))

    sends = []

    def go(copy):
        copy.start()
        sends.append(copy)
        return copy

    first = [[None] * 4 for _ in ORDER]

    def bring(n):
        for i, rel in enumerate(ORDER):
            same, turned = sign * rel, -sign * rel
            src, dst, device = (
                (panel_ref.at[unit_rows(0, 1 - h, turned)], got_a.at[i], sibling),
                (panel_ref.at[small_rows(h, 1 - yl, same)], got_b.at[0, i], partner),
                (panel_ref.at[small_rows(1 - h, 1 - yl, turned)], got_b.at[1, i], diagonal),
                (panel_ref.at[small_rows(1 - h, yl, turned)], got_b.at[2, i], sibling),
            )[n]
            first[i][n] = go(remote(src, dst, first_s.at[n, i], first_r.at[n, i], device))

    for n in range(4):
        bring(n)

    ready = set()

    def masked(u, k, i):
        if (u, i) not in ready:
            ready.add((u, i))
            loads[i][u].wait()
            for copy in first[i][1:] if u else first[i][:1]:
                copy.wait_recv()
        w = weight[k]
        if u == 0:
            return w[0] * own_a[i] + w[3] * got_a[i]
        return w[0] * own_b[i] + w[1] * got_b[0, i] + w[2] * got_b[1, i] + w[3] * got_b[2, i]

    ring = {}

    def sum_step(u, k, s):
        for way, device in ((0, ahead), (1, behind)):
            if s >= HOPS[way]:
                continue
            value = masked(u, k, ORDER.index((HOPS[way] - s) * (1 - 2 * way)))
            if s:
                ring[u, k, way, s - 1].wait_recv()
                value += passed[u][k, way, s - 1]
            mine[u][k, way, s] = value
            ring[u, k, way, s] = go(
                remote(
                    mine[u].at[k, way, s],
                    passed[u].at[k, way, s],
                    rs_s.at[u, k, way, s],
                    rs_r.at[u, k, way, s],
                    device,
                )
            )

    def summed(u, k):
        value = masked(u, k, 7)
        for way in range(2):
            ring[u, k, way, HOPS[way] - 1].wait_recv()
            value += passed[u][k, way, HOPS[way] - 1]
        return value

    def left_of_c(begin, end):
        @pl.loop(begin, end)
        def _(j):
            rows = pl.ds(pl.multiple_of(j * CHUNK, CHUNK), CHUNK)
            high, low = halves(c_v[rows, :].T)
            left_hi[0:WIDTH, rows] = high
            left_lo[0:WIDTH, rows] = low

    beside, spread, side, shared = {}, {}, {}, {}

    def where_of(slot):
        return 0 if slot == 7 else sign * (slot - LONG + 1) if slot >= LONG else -sign * (slot + 1)

    def send_on(copies, key, rows, sems, device):
        k = key[0]
        copies[key] = go(remote(v[k].at[rows], v[k].at[rows], sems[0].at[key], sems[1].at[key], device))

    def share(k, kind, slot):
        where = where_of(slot)
        rows = unit_rows(0, h, where) if kind == 0 else small_rows(h, yl if kind == 1 else 1 - yl, where)
        send_on(shared, (k, kind, slot), rows, (core_s, core_r), sibling)

    def pass_on(k, u, way, s):
        where = -sign * (1 - 2 * way) * s
        rows = small_rows(h, yl, where) if u else unit_rows(0, h, where)
        send_on(spread, (k, u, way, s), rows, (ag_s, ag_r), behind if way else ahead)

    def cross(k, slot):
        send_on(side, (k, slot), small_rows(h, yl, where_of(slot)), (side_s, side_r), partner)

    def offer(k):
        half_a[k] = summed(0, k)
        beside[k] = go(remote(half_a.at[k], other_a.at[k], beside_s.at[k], beside_r.at[k], partner))

    def start(u, k):
        if u:
            v[k][small_rows(h, yl, 0), :] = summed(1, k)
        else:
            beside[k].wait_recv()
            v[k][unit_rows(0, h, 0), :] = half_a[k] + other_a[k]
        for way in range(2):
            pass_on(k, u, way, 0)
        if u:
            cross(k, 7)
        share(k, u, 7)

    def gather(u, k, s):
        for way in range(2):
            if s >= HOPS[way]:
                continue
            spread[k, u, way, s].wait_recv()
            if s + 1 < HOPS[way]:
                pass_on(k, u, way, s + 1)
            slot = way * LONG + s
            if u:
                cross(k, slot)
            share(k, u, slot)

    def slots_of(s):
        return (7,) if s < 0 else (s, LONG + s) if s < SHORT else (s,)

    def crossed(k, s):
        for slot in slots_of(s):
            side[k, slot].wait_recv()
            share(k, 2, slot)

    def products(k, s):
        for kind in range(3):
            for slot in slots_of(s):
                shared[k, kind, slot].wait_recv()
        for way in (1, -1) if 0 <= s < SHORT else (1,):
            rows = group_rows(way * (s + 1))
            value = v[k][rows, :]
            high, low = halves(value)
            v_hi[k, rows, :] = high
            v_lo[k, rows, :] = low
            tall = WIDTH + HALF * k
            if k + 1 < BLOCKS:
                mine_hi, mine_lo = halves(v[k][rows, pl.ds(pl.multiple_of(h * HALF, HALF), HALF)].T)
                left_hi[tall : tall + HALF, rows] = mine_hi
                left_lo[tall : tall + HALF, rows] = mine_lo
            out = dot3((left_hi[0:tall, rows], left_lo[0:tall, rows]), (high, low))
            pieces = [out[0:WIDTH].reshape(8, 32, WIDTH)]
            for b in range(k):
                pieces.append(out[WIDTH + HALF * b : WIDTH + HALF * (b + 1)].reshape(8, 16, WIDTH))
            start = 0
            for piece in pieces:
                stop = start + piece.shape[1]
                if s < 0:
                    part[k][:, start:stop, :] = piece
                else:
                    part[k][:, start:stop, :] += piece
                start = stop

    added, told, exchanged = {}, {}, {}

    def send_parts(k):
        for i, device in enumerate(peers):
            added[k, i] = go(
                remote(part[k].at[device[0]], arrived[k].at[i], row_s.at[k, 0, i], row_r.at[k, 0, i], device)
            )

    def send_sums(k):
        value = part[k][row]
        for i in range(7):
            added[k, i].wait_recv()
            value += arrived[k][i]
        total[k][row] = value
        for i, device in enumerate(peers):
            told[k, i] = go(remote(total[k].at[row], total[k].at[row], row_s.at[k, 1, i], row_r.at[k, 1, i], device))

    def swap_grams(k):
        for i in range(7):
            told[k, i].wait_recv()
        if k:
            src = total[k].at[:, pl.ds(32, 16 * k), :]
            exchanged[k] = go(remote(src, gram[k], gram_s.at[k], gram_r.at[k], sibling))

    def solve(k):
        value = total[k][:, 0:32, :].reshape(WIDTH, WIDTH)
        for b in range(k):
            mine_cols = pl.ds(pl.multiple_of(h * HALF, HALF), HALF)
            value -= dot3(
                (yt_hi[b, :, mine_cols], yt_lo[b, :, mine_cols]),
                halves(total[k][:, 32 + 16 * b : 48 + 16 * b, :].reshape(HALF, WIDTH)),
            )
        if k:
            exchanged[k].wait_recv()
        for b in range(k):
            other_cols = pl.ds(pl.multiple_of((1 - h) * HALF, HALF), HALF)
            value -= dot3(
                (yt_hi[b, :, other_cols], yt_lo[b, :, other_cols]),
                halves(gram[k][:, 16 * b : 16 * b + 16, :].reshape(HALF, WIDTH)),
            )
        value, factor = halves(value), halves(f_v[k])
        high, low = halves(dot3(factor, value, NT))
        y_hi[k] = high
        y_lo[k] = low
        if k + 1 < BLOCKS:
            high, low = halves(dot3(value, factor, NT))
            yt_hi[k] = high
            yt_lo[k] = low

    stores = []

    def update(blocks, last):
        for j in range(ROWS // CHUNK):
            rows = pl.ds(j * CHUNK, CHUNK)
            value = c_v[rows, :]
            for k in blocks:
                value -= dot3((v_hi[k, rows, :], v_lo[k, rows, :]), (y_hi[k], y_lo[k]))
            c_v[rows, :] = value
            if last:
                stores.append(pltpu.make_async_copy(c_v.at[rows], o_ref.at[rows], local_sem.at[2 + j]))
                stores[-1].start()

    def each(step, *args):
        for k in range(BLOCKS):
            step(*args[:1], k, *args[1:])

    A, B = functools.partial(sum_step, 0), functools.partial(sum_step, 1)
    gather_a, gather_b = functools.partial(gather, 0), functools.partial(gather, 1)
    turns = (
        ((A, 0),),
        ((A, 1),),
        ((A, 2),),
        ((A, 3), (B, 0)),
        ((offer,), (B, 1)),
        ((functools.partial(start, 0),), (B, 2)),
        ((gather_a, 0), (B, 3)),
        ((gather_a, 1), (functools.partial(start, 1),)),
        ((gather_a, 2), (gather_b, 0)),
        ((gather_a, 3), (gather_b, 1), (crossed, -1)),
        ((gather_b, 2), (crossed, 0), (products, -1)),
        ((gather_b, 3), (crossed, 1), (products, 0)),
        ((crossed, 2), (products, 1)),
        ((crossed, 3), (products, 2)),
        ((products, 3), (send_parts,)),
        (),
        ((send_sums,),),
    )
    load_c.wait()
    load_f.wait()
    for t in range(len(turns) + max(LAGS)):
        for k in range(BLOCKS):
            if 0 <= t - LAGS[k] < len(turns):
                for step, *args in turns[t - LAGS[k]]:
                    step(k, *args)
            if t == 0 and k < 2:
                left_of_c(2 * k, 2 * k + 2)
    swap_grams(0)
    solve(0)
    swap_grams(1)
    solve(1)
    update((0, 1), False)
    swap_grams(2)
    solve(2)
    update((2,), True)
    for copy in sends:
        copy.wait_send()
    for store in stores:
        store.wait()


def shards(vectors, panels, factors, owners):
    any_space = pl.BlockSpec(memory_space=pl.ANY)
    dma = pltpu.SemaphoreType.DMA
    tall = (ROWS, WIDTH)
    square = (WIDTH, WIDTH)
    return pl.pallas_call(
        kernel,
        out_shape=jax.ShapeDtypeStruct(tall, F32),
        in_specs=[pl.BlockSpec(memory_space=pltpu.SMEM), any_space, any_space, any_space],
        out_specs=any_space,
        scratch_shapes=[
            pltpu.VMEM(tall, F32),
            pltpu.VMEM((BLOCKS, *square), F32),
            pltpu.VMEM((2 * WIDTH, ROWS), BF16),
            pltpu.VMEM((2 * WIDTH, ROWS), BF16),
            *[pltpu.VMEM(tall, F32)] * BLOCKS,
            pltpu.VMEM((BLOCKS, *tall), BF16),
            pltpu.VMEM((BLOCKS, *tall), BF16),
            *[pltpu.VMEM((8, p, WIDTH), F32) for p in PIECES],
            pltpu.VMEM((8, PIECES[0], WIDTH), F32),
            pltpu.VMEM((3, 8, PIECES[1], WIDTH), F32),
            *[pltpu.VMEM((BLOCKS, 2, LONG, p, WIDTH), F32) for p in PIECES],
            *[pltpu.VMEM((BLOCKS, 2, LONG, p, WIDTH), F32) for p in PIECES],
            pltpu.VMEM((BLOCKS, UNIT, WIDTH), F32),
            pltpu.VMEM((BLOCKS, UNIT, WIDTH), F32),
            *[pltpu.VMEM((8, n, WIDTH), F32) for n in SHARES],
            *[pltpu.VMEM((8, n, WIDTH), F32) for n in SHARES],
            *[pltpu.VMEM((7, n, WIDTH), F32) for n in SHARES],
            pltpu.VMEM((8, 16, WIDTH), F32),
            pltpu.VMEM((8, 32, WIDTH), F32),
            *[pltpu.VMEM((BLOCKS, *square), BF16)] * 4,
            dma((18,)),
            dma((4, 8)),
            dma((4, 8)),
            dma((2, BLOCKS, 2, LONG)),
            dma((2, BLOCKS, 2, LONG)),
            dma((BLOCKS,)),
            dma((BLOCKS,)),
            dma((BLOCKS, 2, 2, LONG)),
            dma((BLOCKS, 2, 2, LONG)),
            dma((BLOCKS, 8)),
            dma((BLOCKS, 8)),
            dma((BLOCKS, 3, 8)),
            dma((BLOCKS, 3, 8)),
            dma((BLOCKS, 2, 7)),
            dma((BLOCKS, 2, 7)),
            dma((BLOCKS,)),
            dma((BLOCKS,)),
        ],
        name="back_transform",
        compiler_params=pltpu.CompilerParams(
            collective_id=0, has_side_effects=True, vmem_limit_bytes=60 * 2**20
        ),
    )(owners, vectors, panels[0], factors)


def solution(mesh):
    placed = (P("row", "col"), P("col", "row", None), P(), P())
    return jax.shard_map(shards, mesh=mesh, in_specs=placed, out_specs=P("row", "col"), check_vma=False)
```

time: 562 us -> 109 us (0.19)
  waiting for transfers between devices: 503 us -> 0 us
  Pallas kernels: 0 us -> 106 us
  matrix products: 31.7 us -> 0 us
  between operations: 15.1 us -> 0.01 us
    psum x4 -> x0, waiting for transfers between devices: 503 us -> none  [the longest x3 258 us: shards(): projected = lax.psum(inner(reflector, current), 'row')]
    pallas_call x0 -> x1, Pallas kernels: none -> 106 us  [shards(): pl.pallas_call(kernel, out_shape=jax.ShapeDtypeStruct(tall, F32), in_spec...]
    dot_general x9 -> x0, matrix products: 31.7 us -> none  [the longest x6 17.2 us: matmul(): jnp.dot(left, right, precision=lax.Precision.HIGHEST, preferred_element_t...]
  transfers between devices with their start and end apart: 4 -> 0, of which waited for: 4 -> 0; matrix products, arithmetic and copies ran while one was open for 0% -> 0% of each run, Pallas kernels for 0% -> 0%
where the time goes in v1:
time: 109 us
  Pallas kernels  106 us (97%)
  local copies, waits for them, and re-layouts  3.05 us (3%)
    pallas_call x1, Pallas kernels, shards(): pl.pallas_call(kernel, out_shape=jax.ShapeDtypeStruct(tall, F32), in_spec...  106 us
    unnamed x1, local copies, waits for them, and re-layouts  3.05 us

profile of v1, /device:TPU:1, one launch (start us, length us, event | category | flops | bytes accessed | tf_op | source)
XLA Modules:
  0.0 109.3 jit_solution(3381151418242320178)
XLA Ops:
  0.0 106.2 %back_transform.1 = f32[2048,256]{1,0:T(8,128)} custom-call(s32[3]{0:T(128)} %owners.1, f32[2048,256]{1,0:T(8,128)} %c_ref.1, f32[2048,256]{1,0:T(8,128)} %bitcast.1, f32[3,256,256]{2,1,0:T(8,128)} %factors_ref.1), custom_call_target="tpu_custom_call" | custom-call | tf_op jit(solution)/shard_map/back_transform/pallas_call | solution.py:381
  106.2 3.0 %copy.6 = f32[2048,256]{1,0:T(8,128)} copy(f32[2048,256]{1,0:T(8,128)} %back_transform.1) | data formatting | bytes 4194304

commit v2 on v1

--- a/solution.py
+++ b/solution.py
@@ -20,7 +20,10 @@
 ORDER = (4, -3, 3, -2, 2, -1, 1, 0)
 LONG, SHORT = 4, 3
 HOPS = (LONG, SHORT)
-SHARES = (32, 48, 64)
+SHARE = 32
+STRIP = 16
+PAIRS = ((0, 1), (0, 2), (1, 2))
+TILE = 8
 LAGS = (0, 0, 0)
 NN = (((1,), (0,)), ((), ()))
 NT = (((1,), (1,)), ((), ()))
@@ -42,12 +45,11 @@
     owners, c_ref, panel_ref, factors_ref, o_ref,
     c_v, f_v, left_hi, left_lo, v0, v1, v2, v_hi, v_lo,
     own_a, own_b, got_a, got_b, mine_a, mine_b, passed_a, passed_b, half_a, other_a,
-    part0, part1, part2, sum0, sum1, sum2, in0, in1, in2, gram1, gram2, yt_hi, yt_lo, y_hi, y_lo,
+    part, total, arrived, turned, strip, strip_in, strip_sum, gram, yt_hi, yt_lo, y_hi, y_lo,
     local_sem, first_s, first_r, rs_s, rs_r, beside_s, beside_r, ag_s, ag_r, side_s, side_r, core_s, core_r, row_s, row_r,
-    gram_s, gram_r,
+    strip_s, strip_r, plane_s, plane_r, gram_s, gram_r,
 ):
-    v, part, total, arrived = (v0, v1, v2), (part0, part1, part2), (sum0, sum1, sum2), (in0, in1, in2)
-    gram = (None, gram1, gram2)
+    v = (v0, v1, v2)
     mine, passed = (mine_a, mine_b), (passed_a, passed_b)
     row, col = lax.axis_index("row"), lax.axis_index("col")
     yh, x = row // 4, row % 4
@@ -80,7 +82,8 @@
     peers = [((yh ^ (i // 4)) * 4 + (x + i % 4) % 4, col) for i in range(1, 8)]
 
     barrier = pltpu.get_barrier_semaphore()
-    everyone = [sibling, partner, diagonal, ahead, behind] + peers
+    mates = [at(0, i, 0) for i in range(1, 8)]
+    everyone = [sibling, partner, diagonal] + mates + peers
     for device in everyone:
         pl.semaphore_signal(barrier, inc=1, device_id=device, device_id_type=MESH)
 
@@ -245,64 +248,80 @@
             high, low = halves(value)
             v_hi[k, rows, :] = high
             v_lo[k, rows, :] = low
-            tall = WIDTH + HALF * k
+            tall = WIDTH + STRIP * k
             if k + 1 < BLOCKS:
-                mine_hi, mine_lo = halves(v[k][rows, pl.ds(pl.multiple_of(h * HALF, HALF), HALF)].T)
-                left_hi[tall : tall + HALF, rows] = mine_hi
-                left_lo[tall : tall + HALF, rows] = mine_lo
+                turned[...] = v[k][rows, pl.ds(pl.multiple_of(h * HALF, HALF), HALF)].T
+                mine_hi, mine_lo = halves(turned[pl.ds(pl.multiple_of(z * STRIP, STRIP), STRIP), :])
+                left_hi[tall : tall + STRIP, rows] = mine_hi
+                left_lo[tall : tall + STRIP, rows] = mine_lo
             out = dot3((left_hi[0:tall, rows], left_lo[0:tall, rows]), (high, low))
-            pieces = [out[0:WIDTH].reshape(8, 32, WIDTH)]
+            pieces = [(part.at[k], out[0:WIDTH].reshape(8, SHARE, WIDTH))]
             for b in range(k):
-                pieces.append(out[WIDTH + HALF * b : WIDTH + HALF * (b + 1)].reshape(8, 16, WIDTH))
-            start = 0
-            for piece in pieces:
-                stop = start + piece.shape[1]
+                n = PAIRS.index((b, k))
+                begin = WIDTH + STRIP * b
+                pieces.append((strip.at[2 * n : 2 * n + 2], out[begin : begin + STRIP].reshape(2, TILE, WIDTH)))
+            for ref, piece in pieces:
                 if s < 0:
-                    part[k][:, start:stop, :] = piece
+                    ref[...] = piece
                 else:
-                    part[k][:, start:stop, :] += piece
-                start = stop
-
-    added, told, exchanged = {}, {}, {}
+                    ref[...] += piece
+
+    added, told, strips, planes = {}, {}, {}, {}
 
     def send_parts(k):
         for i, device in enumerate(peers):
             added[k, i] = go(
-                remote(part[k].at[device[0]], arrived[k].at[i], row_s.at[k, 0, i], row_r.at[k, 0, i], device)
+                remote(part.at[k, device[0]], arrived.at[k, i], row_s.at[k, 0, i], row_r.at[k, 0, i], device)
             )
 
     def send_sums(k):
-        value = part[k][row]
+        value = part[k, row]
         for i in range(7):
             added[k, i].wait_recv()
-            value += arrived[k][i]
-        total[k][row] = value
+            value += arrived[k, i]
+        total[k, row] = value
         for i, device in enumerate(peers):
-            told[k, i] = go(remote(total[k].at[row], total[k].at[row], row_s.at[k, 1, i], row_r.at[k, 1, i], device))
-
-    def swap_grams(k):
+            told[k, i] = go(remote(total.at[k, row], total.at[k, row], row_s.at[k, 1, i], row_r.at[k, 1, i], device))
+
+    def send_strips():
+        strip[6:8] = jnp.zeros((2, TILE, WIDTH), F32)
+        for i, device in enumerate(peers):
+            strips[0, i] = go(remote(strip.at[device[0]], strip_in.at[i], strip_s.at[0, i], strip_r.at[0, i], device))
+
+    def send_strip_sums():
+        value = strip[row]
+        for i in range(7):
+            strips[0, i].wait_recv()
+            value += strip_in[i]
+        strip_sum[row] = value
+        for i, device in enumerate(peers):
+            strips[1, i] = go(
+                remote(strip_sum.at[row], strip_sum.at[row], strip_s.at[1, i], strip_r.at[1, i], device)
+            )
+
+    def spread_grams():
+        for i in range(7):
+            strips[1, i].wait_recv()
+        gram[h, z] = strip_sum[0:6]
+        for i, device in enumerate(mates):
+            planes[i] = go(remote(gram.at[h, z], gram.at[h, z], plane_s.at[i], plane_r.at[i], device))
+
+    def swap_grams():
+        for i in range(7):
+            planes[i].wait_recv()
+        planes[7] = go(remote(gram.at[h], gram.at[h], gram_s, gram_r, sibling))
+
+    def solve(k):
         for i in range(7):
             told[k, i].wait_recv()
-        if k:
-            src = total[k].at[:, pl.ds(32, 16 * k), :]
-            exchanged[k] = go(remote(src, gram[k], gram_s.at[k], gram_r.at[k], sibling))
-
-    def solve(k):
-        value = total[k][:, 0:32, :].reshape(WIDTH, WIDTH)
+        value = total[k].reshape(WIDTH, WIDTH)
         for b in range(k):
-            mine_cols = pl.ds(pl.multiple_of(h * HALF, HALF), HALF)
-            value -= dot3(
-                (yt_hi[b, :, mine_cols], yt_lo[b, :, mine_cols]),
-                halves(total[k][:, 32 + 16 * b : 48 + 16 * b, :].reshape(HALF, WIDTH)),
-            )
-        if k:
-            exchanged[k].wait_recv()
-        for b in range(k):
-            other_cols = pl.ds(pl.multiple_of((1 - h) * HALF, HALF), HALF)
-            value -= dot3(
-                (yt_hi[b, :, other_cols], yt_lo[b, :, other_cols]),
-                halves(gram[k][:, 16 * b : 16 * b + 16, :].reshape(HALF, WIDTH)),
-            )
+            n = PAIRS.index((b, k))
+            for half in range(2):
+                value -= dot3(
+                    (yt_hi[b, :, half * HALF : (half + 1) * HALF], yt_lo[b, :, half * HALF : (half + 1) * HALF]),
+                    halves(gram[half, :, 2 * n : 2 * n + 2].reshape(HALF, WIDTH)),
+                )
         value, factor = halves(value), halves(f_v[k])
         high, low = halves(dot3(factor, value, NT))
         y_hi[k] = high
@@ -346,9 +365,7 @@
         ((gather_b, 3), (crossed, 1), (products, 0)),
         ((crossed, 2), (products, 1)),
         ((crossed, 3), (products, 2)),
-        ((products, 3), (send_parts,)),
-        (),
-        ((send_sums,),),
+        ((products, 3),),
     )
     load_c.wait()
     load_f.wait()
@@ -359,14 +376,19 @@
                     step(k, *args)
             if t == 0 and k < 2:
                 left_of_c(2 * k, 2 * k + 2)
-    swap_grams(0)
+    send_strips()
+    for k in range(BLOCKS):
+        send_parts(k)
+    send_strip_sums()
+    spread_grams()
+    for k in range(BLOCKS):
+        send_sums(k)
+    swap_grams()
     solve(0)
-    swap_grams(1)
+    planes[7].wait_recv()
     solve(1)
-    update((0, 1), False)
-    swap_grams(2)
     solve(2)
-    update((2,), True)
+    update((0, 1, 2), True)
     for copy in sends:
         copy.wait_send()
     for store in stores:
@@ -398,11 +420,14 @@
             *[pltpu.VMEM((BLOCKS, 2, LONG, p, WIDTH), F32) for p in PIECES],
             pltpu.VMEM((BLOCKS, UNIT, WIDTH), F32),
             pltpu.VMEM((BLOCKS, UNIT, WIDTH), F32),
-            *[pltpu.VMEM((8, n, WIDTH), F32) for n in SHARES],
-            *[pltpu.VMEM((8, n, WIDTH), F32) for n in SHARES],
-            *[pltpu.VMEM((7, n, WIDTH), F32) for n in SHARES],
-            pltpu.VMEM((8, 16, WIDTH), F32),
-            pltpu.VMEM((8, 32, WIDTH), F32),
+            pltpu.VMEM((BLOCKS, 8, SHARE, WIDTH), F32),
+            pltpu.VMEM((BLOCKS, 8, SHARE, WIDTH), F32),
+            pltpu.VMEM((BLOCKS, 7, SHARE, WIDTH), F32),
+            pltpu.VMEM((HALF, WIDTH), F32),
+            pltpu.VMEM((8, TILE, WIDTH), F32),
+            pltpu.VMEM((7, TILE, WIDTH), F32),
+            pltpu.VMEM((8, TILE, WIDTH), F32),
+            pltpu.VMEM((2, 8, 6, TILE, WIDTH), F32),
             *[pltpu.VMEM((BLOCKS, *square), BF16)] * 4,
             dma((18,)),
             dma((4, 8)),
@@ -419,8 +444,12 @@
             dma((BLOCKS, 3, 8)),
             dma((BLOCKS, 2, 7)),
             dma((BLOCKS, 2, 7)),
-            dma((BLOCKS,)),
-            dma((BLOCKS,)),
+            dma((2, 7)),
+            dma((2, 7)),
+            dma((7,)),
+            dma((7,)),
+            dma,
+            dma,
         ],
         name="back_transform",
         compiler_params=pltpu.CompilerParams(

time: 109 us -> 109 us (level)
  no operation moved by 1% of the time
where the time goes in v2:
time: 109 us; the launch traced here: 108 us
  Pallas kernels  105 us (96%)
  local copies, waits for them, and re-layouts  3.05 us (3%)
    pallas_call x1, Pallas kernels, shards(): pl.pallas_call(kernel, out_shape=jax.ShapeDtypeStruct(tall, F32), in_spec...  105 us
    unnamed x1, local copies, waits for them, and re-layouts  3.05 us

profile of v2, /device:TPU:1, one launch (start us, length us, event | category | flops | bytes accessed | tf_op | source)
XLA Modules:
  0.0 108.5 jit_solution(8175196860777725225)
XLA Ops:
  0.0 105.4 %back_transform.1 = f32[2048,256]{1,0:T(8,128)} custom-call(s32[3]{0:T(128)} %owners.1, f32[2048,256]{1,0:T(8,128)} %c_ref.1, f32[2048,256]{1,0:T(8,128)} %bitcast.1, f32[3,256,256]{2,1,0:T(8,128)} %factors_ref.1), custom_call_target="tpu_custom_call" | custom-call | tf_op jit(solution)/shard_map/back_transform/pallas_call | solution.py:403
  105.4 3.0 %copy.6 = f32[2048,256]{1,0:T(8,128)} copy(f32[2048,256]{1,0:T(8,128)} %back_transform.1) | data formatting | bytes 4194304

commit v3 on v2

--- a/solution.py
+++ b/solution.py
@@ -24,7 +24,6 @@
 STRIP = 16
 PAIRS = ((0, 1), (0, 2), (1, 2))
 TILE = 8
-LAGS = (0, 0, 0)
 NN = (((1,), (0,)), ((), ()))
 NT = (((1,), (1,)), ((), ()))
 
@@ -45,7 +44,7 @@
     owners, c_ref, panel_ref, factors_ref, o_ref,
     c_v, f_v, left_hi, left_lo, v0, v1, v2, v_hi, v_lo,
     own_a, own_b, got_a, got_b, mine_a, mine_b, passed_a, passed_b, half_a, other_a,
-    part, total, arrived, turned, strip, strip_in, strip_sum, gram, yt_hi, yt_lo, y_hi, y_lo,
+    part, total, arrived, strip, strip_in, tile, tile_in, tile_sum, gram, yt_hi, yt_lo, y_hi, y_lo,
     local_sem, first_s, first_r, rs_s, rs_r, beside_s, beside_r, ag_s, ag_r, side_s, side_r, core_s, core_r, row_s, row_r,
     strip_s, strip_r, plane_s, plane_r, gram_s, gram_r,
 ):
@@ -248,23 +247,11 @@
             high, low = halves(value)
             v_hi[k, rows, :] = high
             v_lo[k, rows, :] = low
-            tall = WIDTH + STRIP * k
-            if k + 1 < BLOCKS:
-                turned[...] = v[k][rows, pl.ds(pl.multiple_of(h * HALF, HALF), HALF)].T
-                mine_hi, mine_lo = halves(turned[pl.ds(pl.multiple_of(z * STRIP, STRIP), STRIP), :])
-                left_hi[tall : tall + STRIP, rows] = mine_hi
-                left_lo[tall : tall + STRIP, rows] = mine_lo
-            out = dot3((left_hi[0:tall, rows], left_lo[0:tall, rows]), (high, low))
-            pieces = [(part.at[k], out[0:WIDTH].reshape(8, SHARE, WIDTH))]
-            for b in range(k):
-                n = PAIRS.index((b, k))
-                begin = WIDTH + STRIP * b
-                pieces.append((strip.at[2 * n : 2 * n + 2], out[begin : begin + STRIP].reshape(2, TILE, WIDTH)))
-            for ref, piece in pieces:
-                if s < 0:
-                    ref[...] = piece
-                else:
-                    ref[...] += piece
+            out = dot3((left_hi[:, rows], left_lo[:, rows]), (high, low)).reshape(8, SHARE, WIDTH)
+            if s < 0:
+                part[k] = out
+            else:
+                part[k] += out
 
     added, told, strips, planes = {}, {}, {}, {}
 
@@ -284,32 +271,51 @@
             told[k, i] = go(remote(total.at[k, row], total.at[k, row], row_s.at[k, 1, i], row_r.at[k, 1, i], device))
 
     def send_strips():
-        strip[6:8] = jnp.zeros((2, TILE, WIDTH), F32)
+        rows = group_rows(0)
+        cols = pl.ds(pl.multiple_of(h * HALF, HALF), HALF)
+        left = [halves(v[b][rows, cols].T) for b in range(BLOCKS - 1)]
+        for n, (b, k) in enumerate(PAIRS):
+            out = dot3(left[b], (v_hi[k, rows, :], v_lo[k, rows, :]))
+            strip[:, STRIP * n : STRIP * (n + 1), :] = out.reshape(8, STRIP, WIDTH)
         for i, device in enumerate(peers):
             strips[0, i] = go(remote(strip.at[device[0]], strip_in.at[i], strip_s.at[0, i], strip_r.at[0, i], device))
 
-    def send_strip_sums():
+    def send_tiles():
         value = strip[row]
         for i in range(7):
             strips[0, i].wait_recv()
             value += strip_in[i]
-        strip_sum[row] = value
+        tile[0:6] = value.reshape(6, TILE, WIDTH)
+        tile[6:8] = jnp.zeros((2, TILE, WIDTH), F32)
+        for i, device in enumerate(mates):
+            planes[0, i] = go(
+                remote(tile.at[along(i + 1)], tile_in.at[i], plane_s.at[0, i], plane_r.at[0, i], device)
+            )
+
+    def send_tile_sums():
+        value = tile[z]
+        for i in range(7):
+            planes[0, i].wait_recv()
+            value += tile_in[i]
+        tile_sum[z] = value
+        for i, device in enumerate(mates):
+            planes[1, i] = go(
+                remote(tile_sum.at[z], tile_sum.at[z], plane_s.at[1, i], plane_r.at[1, i], device)
+            )
+
+    def spread_grams():
+        for i in range(7):
+            planes[1, i].wait_recv()
+        gram[h, row] = tile_sum[0:6]
         for i, device in enumerate(peers):
             strips[1, i] = go(
-                remote(strip_sum.at[row], strip_sum.at[row], strip_s.at[1, i], strip_r.at[1, i], device)
-            )
-
-    def spread_grams():
+                remote(gram.at[h, row], gram.at[h, row], strip_s.at[1, i], strip_r.at[1, i], device)
+            )
+
+    def swap_grams():
         for i in range(7):
             strips[1, i].wait_recv()
-        gram[h, z] = strip_sum[0:6]
-        for i, device in enumerate(mates):
-            planes[i] = go(remote(gram.at[h, z], gram.at[h, z], plane_s.at[i], plane_r.at[i], device))
-
-    def swap_grams():
-        for i in range(7):
-            planes[i].wait_recv()
-        planes[7] = go(remote(gram.at[h], gram.at[h], gram_s, gram_r, sibling))
+        planes[2] = go(remote(gram.at[h], gram.at[h], gram_s, gram_r, sibling))
 
     def solve(k):
         for i in range(7):
@@ -359,33 +365,31 @@
         ((functools.partial(start, 0),), (B, 2)),
         ((gather_a, 0), (B, 3)),
         ((gather_a, 1), (functools.partial(start, 1),)),
-        ((gather_a, 2), (gather_b, 0)),
-        ((gather_a, 3), (gather_b, 1), (crossed, -1)),
-        ((gather_b, 2), (crossed, 0), (products, -1)),
+        ((gather_a, 2), (gather_b, 0), (crossed, -1)),
+        ((gather_a, 3), (gather_b, 1), (products, -1)),
+        ((gather_b, 2), (crossed, 0)),
         ((gather_b, 3), (crossed, 1), (products, 0)),
         ((crossed, 2), (products, 1)),
         ((crossed, 3), (products, 2)),
-        ((products, 3),),
+        ((products, 3), (send_parts,)),
     )
     load_c.wait()
     load_f.wait()
-    for t in range(len(turns) + max(LAGS)):
+    aside = {9: send_strips, 13: send_tiles, 14: send_tile_sums}
+    for t, turn in enumerate(turns):
         for k in range(BLOCKS):
-            if 0 <= t - LAGS[k] < len(turns):
-                for step, *args in turns[t - LAGS[k]]:
-                    step(k, *args)
+            for step, *args in turn:
+                step(k, *args)
             if t == 0 and k < 2:
                 left_of_c(2 * k, 2 * k + 2)
-    send_strips()
-    for k in range(BLOCKS):
-        send_parts(k)
-    send_strip_sums()
+        if t in aside:
+            aside[t]()
     spread_grams()
     for k in range(BLOCKS):
         send_sums(k)
     swap_grams()
     solve(0)
-    planes[7].wait_recv()
+    planes[2].wait_recv()
     solve(1)
     solve(2)
     update((0, 1, 2), True)
@@ -408,8 +412,8 @@
         scratch_shapes=[
             pltpu.VMEM(tall, F32),
             pltpu.VMEM((BLOCKS, *square), F32),
-            pltpu.VMEM((2 * WIDTH, ROWS), BF16),
-            pltpu.VMEM((2 * WIDTH, ROWS), BF16),
+            pltpu.VMEM((WIDTH, ROWS), BF16),
+            pltpu.VMEM((WIDTH, ROWS), BF16),
             *[pltpu.VMEM(tall, F32)] * BLOCKS,
             pltpu.VMEM((BLOCKS, *tall), BF16),
             pltpu.VMEM((BLOCKS, *tall), BF16),
@@ -423,7 +427,8 @@
             pltpu.VMEM((BLOCKS, 8, SHARE, WIDTH), F32),
             pltpu.VMEM((BLOCKS, 8, SHARE, WIDTH), F32),
             pltpu.VMEM((BLOCKS, 7, SHARE, WIDTH), F32),
-            pltpu.VMEM((HALF, WIDTH), F32),
+            pltpu.VMEM((8, 3 * STRIP, WIDTH), F32),
+            pltpu.VMEM((7, 3 * STRIP, WIDTH), F32),
             pltpu.VMEM((8, TILE, WIDTH), F32),
             pltpu.VMEM((7, TILE, WIDTH), F32),
             pltpu.VMEM((8, TILE, WIDTH), F32),
@@ -446,8 +451,8 @@
             dma((BLOCKS, 2, 7)),
             dma((2, 7)),
             dma((2, 7)),
-            dma((7,)),
-            dma((7,)),
+            dma((2, 7)),
+            dma((2, 7)),
             dma,
             dma,
         ],

time: 109 us -> 108 us (level)
    pallas_call x1, Pallas kernels: 105 us -> 104 us  [shards(): pl.pallas_call(kernel, out_shape=jax.ShapeDtypeStruct(tall, F32), in_spec...]
where the time goes in v3:
time: 108 us; the launch traced here: 107 us
  Pallas kernels  104 us (96%)
  local copies, waits for them, and re-layouts  3.05 us (3%)
    pallas_call x1, Pallas kernels, shards(): pl.pallas_call(kernel, out_shape=jax.ShapeDtypeStruct(tall, F32), in_spec...  104 us
    unnamed x1, local copies, waits for them, and re-layouts  3.05 us

profile of v3, /device:TPU:1, one launch (start us, length us, event | category | flops | bytes accessed | tf_op | source)
XLA Modules:
  0.0 106.8 jit_solution(3339270583907305040)
XLA Ops:
  0.0 103.8 %back_transform.1 = f32[2048,256]{1,0:T(8,128)} custom-call(s32[3]{0:T(128)} %owners.1, f32[2048,256]{1,0:T(8,128)} %c_ref.1, f32[2048,256]{1,0:T(8,128)} %bitcast.1, f32[3,256,256]{2,1,0:T(8,128)} %factors_ref.1), custom_call_target="tpu_custom_call" | custom-call | tf_op jit(solution)/shard_map/back_transform/pallas_call | solution.py:407
  103.8 3.0 %copy.6 = f32[2048,256]{1,0:T(8,128)} copy(f32[2048,256]{1,0:T(8,128)} %back_transform.1) | data formatting | bytes 4194304

commit v4 on v3

--- a/solution.py
+++ b/solution.py
@@ -391,8 +391,9 @@
     solve(0)
     planes[2].wait_recv()
     solve(1)
+    update((0, 1), False)
     solve(2)
-    update((0, 1, 2), True)
+    update((2,), True)
     for copy in sends:
         copy.wait_send()
     for store in stores:

time: 108 us -> 108 us (level)
  no operation moved by 1% of the time
where the time goes in v4:
time: 108 us; the launch traced here: 107 us
  Pallas kernels  104 us (96%)
  local copies, waits for them, and re-layouts  3.05 us (3%)
    pallas_call x1, Pallas kernels, shards(): pl.pallas_call(kernel, out_shape=jax.ShapeDtypeStruct(tall, F32), in_spec...  104 us
    unnamed x1, local copies, waits for them, and re-layouts  3.05 us

profile of v4, /device:TPU:1, one launch (start us, length us, event | category | flops | bytes accessed | tf_op | source)
XLA Modules:
  0.0 106.8 jit_solution(1578251620339957514)
XLA Ops:
  0.0 103.7 %back_transform.1 = f32[2048,256]{1,0:T(8,128)} custom-call(s32[3]{0:T(128)} %owners.1, f32[2048,256]{1,0:T(8,128)} %c_ref.1, f32[2048,256]{1,0:T(8,128)} %bitcast.1, f32[3,256,256]{2,1,0:T(8,128)} %factors_ref.1), custom_call_target="tpu_custom_call" | custom-call | tf_op jit(solution)/shard_map/back_transform/pallas_call | solution.py:408
  103.7 3.0 %copy.6 = f32[2048,256]{1,0:T(8,128)} copy(f32[2048,256]{1,0:T(8,128)} %back_transform.1) | data formatting | bytes 4194304
